TPU v7x, 32 devices: a whole 2x2x4 slice. The times are simulated.
32 devices in a mesh: replica: 4 (over y, core), shard: 8 (over z, x).
Axes of the slice: x: 2, y: 2, z: 4, core: 2. Of those that a mesh axis runs over, the one named last changes fastest.
Arguments:
- tokens_in: bfloat16 [4096, 8192], P(('replica', 'shard')), may hold values from -6 to 6
- cotangent: bfloat16 [4096, 128], P(('replica', 'shard')), may hold values from -0.1875 to 0.1875
- next_tokens: bfloat16 [2048, 8192], P(('replica', 'shard')), may hold values from -6 to 6
- master: float32 [8192, 128], P(('replica', 'shard')), may hold values from -0.0625 to 0.0625
- first_moment: float32 [8192, 128], P(('replica', 'shard')), may hold values from -6 to 6
- second_moment: float32 [8192, 128], P(('replica', 'shard')), may hold values from 0.25 to 4
Outputs:
- new_master: float32 [8192, 128], P(('replica', 'shard'))
- new_first: float32 [8192, 128], P(('replica', 'shard'))
- new_second: float32 [8192, 128], P(('replica', 'shard'))
- next_out: bfloat16 [2048, 128], P(('replica', 'shard'))
All inputs are finite; a program needn't handle non-finite values.
Results may differ from a plain program's by a relative error of at most 0.005.
Values may be sent and summed in bfloat16 or wider, within the bound.
A program may use at most 64 MiB of HBM per device.

v0:
```python
import jax
import jax.numpy as jnp
from jax import lax
from jax.sharding import PartitionSpec as P

beta_one = 0.9
beta_two = 0.95
learn_rate = 0.003
decay_rate = 0.1
epsilon = 1e-08
steps_done = 10


def on_device(tokens_in, cotangent, next_tokens, master, first_moment, second_moment):
    n_rep = lax.axis_size("replica")
    n_shard = lax.axis_size("shard")
    model_width = tokens_in.shape[1]
    own_rows = model_width // (n_rep * n_shard)
    blocked = lax.psum_scatter(
        lax.dot_general(
            tokens_in, cotangent, (((0,), (0,)), ((), ())), preferred_element_type=jnp.float32
        ),
        "replica",
        scatter_dimension=0,
        tiled=True,
    )
    gradient = lax.psum_scatter(blocked, "shard", scatter_dimension=0, tiled=True)
    new_first = beta_one * first_moment + (1.0 - beta_one) * gradient
    new_second = beta_two * second_moment + (1.0 - beta_two) * gradient * gradient
    first_hat = new_first / (1.0 - beta_one**steps_done)
    second_hat = new_second / (1.0 - beta_two**steps_done)
    new_master = master - learn_rate * (
        first_hat / (jnp.sqrt(second_hat) + epsilon) + decay_rate * master
    )
    low_weight = new_master.astype(jnp.bfloat16)
    group_rows = lax.all_gather(low_weight, "replica", axis=0, tiled=True)
    row_count = next_tokens.shape[0]
    arranged = next_tokens.reshape(row_count, n_rep, n_shard, own_rows).transpose(0, 2, 1, 3)
    columns = arranged.reshape(row_count, model_width)
    summed = jnp.dot(
        columns,
        lax.all_gather(group_rows, "shard", axis=0, tiled=True),
        preferred_element_type=jnp.float32,
    )
    next_out = summed.astype(jnp.bfloat16)
    return (new_master, new_first, new_second, next_out)


def solution(mesh):
    in_specs = (
        P(("replica", "shard"), None),
        P(("replica", "shard"), None),
        P(("replica", "shard"), None),
        P(("replica", "shard"), None),
        P(("replica", "shard"), None),
        P(("replica", "shard"), None),
    )
    out_specs = (
        P(("replica", "shard"), None),
        P(("replica", "shard"), None),
        P(("replica", "shard"), None),
        P(("replica", "shard"), None),
    )
    return jax.shard_map(
        on_device, mesh=mesh, in_specs=in_specs, out_specs=out_specs, check_vma=False
    )
```

profile of v0, /device:TPU:0, one launch (start us, length us, event | category | flops | bytes accessed | tf_op | source)
XLA Modules:
  0.0 192.6 jit_solution(4871367616220754912)
XLA Ops:
  7.2 0.0 copy-start
  7.2 0.0 reduce-scatter.3.cloned.1.call-start
  7.2 1.5 copy-done
  8.8 3.5 %fusion.4 = f32[8192,128]{1,0:T(8,128)} fusion(bf16[128,8192]{1,0:T(8,128)(2,1)S(1)} %copy-done, bf16[128,128]{1,0:T(8,128)(2,1)} %param.7), kind=kOutput, calls=%fused_computation.8 | convolution fusion | flops 268435456 | bytes 6324224 | tf_op jit(solution)/shard_map/dot_general | solution.py:20
  12.2 0.0 copy-start.2
  12.2 0.0 reduce-scatter.3.cloned.1.call-update
  12.2 0.0 copy-start.1
  12.3 0.0 reduce-scatter.5.cloned.1.call-start
  12.3 47.3 %reduce-scatter.3.cloned.1.call-done = f32[2048,128]{1,0:T(8,128)} async-done(((f32[8192,128]{1,0:T(8,128)}), f32[2048,128]{1,0:T(8,128)}) %reduce-scatter.3.cloned.1.call-update) | async-done | bytes 1048592 | tf_op jit(solution)/shard_map/reduce_scatter | solution.py:19
  59.6 0.0 reduce-scatter.5.cloned.1.call-update
  59.6 0.0 all-gather.2.cloned.1.call-start
  59.7 67.2 %reduce-scatter.5.cloned.1.call-done = f32[256,128]{1,0:T(8,128)} async-done(((f32[2048,128]{1,0:T(8,128)}), f32[256,128]{1,0:T(8,128)}) %reduce-scatter.5.cloned.1.call-update) | async-done | bytes 131088 | tf_op jit(solution)/shard_map/reduce_scatter | solution.py:27
  126.9 0.0 copy-done.2
  126.9 0.0 copy-done.3
  126.9 0.0 copy-done.4
  126.9 1.7 fusion.2
  128.6 6.2 %all_gather.6 = bf16[1024,128]{1,0:T(8,128)(2,1)} all-gather(bf16[256,128]{1,0:T(8,128)(2,1)S(1)} %get-tuple-element.4), channel_id=1, replica_groups=mesh['replica'=4,'shard'=8] {'replica'}, dimensions={0}, use_global_device_ids=true | all-gather | bytes 327680 | tf_op jit(solution)/shard_map/all_gather | solution.py:36
  134.8 0.0 all-gather.2.cloned.1.call-update
  134.9 0.0 copy-done.1
  134.9 0.3 copy.11
  135.1 1.5 copy.13
  136.7 1.8 reshape.15
  138.5 44.9 %all-gather.2.cloned.1.call-done = bf16[8192,128]{1,0:T(8,128)(2,1)} async-done(((bf16[1024,128]{1,0:T(8,128)(2,1)}), bf16[8192,128]{1,0:T(8,128)(2,1)}) %all-gather.2.cloned.1.call-update) | async-done | bytes 2097168 | tf_op jit(solution)/shard_map/all_gather | solution.py:42
  183.4 2.7 %fusion = bf16[64,128]{1,0:T(8,128)(2,1)} fusion(bf16[64,8192]{1,0:T(8,128)(2,1)S(1)} %reshape.15, bf16[8192,128]{1,0:T(8,128)(2,1)} %all-gather.2.cloned.1.call-done), kind=kOutput, calls=%fused_computation.1 | convolution fusion | flops 134225920 | bytes 3162112 | tf_op jit(solution)/shard_map/dot_general | solution.py:40
  (2 shorter events, 0.0 us)
Async XLA Ops:
  7.2 1.6 copy-start
  7.2 52.4 %reduce-scatter.3.cloned.1.call-start = ((), (), s32[]{:S(2)}) async-start(), calls=%async_computation.2 | async-start | bytes 5242880 | tf_op jit(solution)/shard_map/reduce_scatter | solution.py:19
  12.2 114.7 %copy-start.2 = (f32[256,128]{1,0:T(8,128)S(1)}, f32[256,128]{1,0:T(8,128)}, u32[]{:S(2)}) copy-start(f32[256,128]{1,0:T(8,128)} %param.9) | copy-start | bytes 393220
  12.2 114.7 %copy-start.3 = (f32[256,128]{1,0:T(8,128)S(1)}, f32[256,128]{1,0:T(8,128)}, u32[]{:S(2)}) copy-start(f32[256,128]{1,0:T(8,128)} %param.10) | copy-start | bytes 393220
  12.2 114.7 %copy-start.4 = (f32[256,128]{1,0:T(8,128)S(1)}, f32[256,128]{1,0:T(8,128)}, u32[]{:S(2)}) copy-start(f32[256,128]{1,0:T(8,128)} %param.11) | copy-start | bytes 393220
  12.2 122.6 %copy-start.1 = (bf16[64,8192]{1,0:T(8,128)(2,1)S(1)}, bf16[64,8192]{1,0:T(8,128)(2,1)}, u32[]{:S(2)}) copy-start(bf16[64,8192]{1,0:T(8,128)(2,1)} %param.8) | copy-start | bytes 3145732
  12.3 114.7 %reduce-scatter.5.cloned.1.call-start = ((), (), s32[]{:S(2)}) async-start(), calls=%async_computation.3 | async-start | bytes 1179648 | tf_op jit(solution)/shard_map/reduce_scatter | solution.py:27
  59.6 123.7 %all-gather.2.cloned.1.call-start = ((), (), s32[]{:S(2)}) async-start(), calls=%async_computation.4 | async-start | bytes 2359296 | tf_op jit(solution)/shard_map/all_gather | solution.py:42
Sparse Core Ops, SparseCore 0:
  12.4 47.2 reduce-scatter.2
  63.4 63.4 reduce-scatter.4
  135.0 48.3 all-gather.1
where the time goes:
time: 193 us
  waiting for transfers between devices  159 us (82%)
  between operations  13.8 us (7%)
  blocking collectives  6.22 us (3%)
  matrix products  6.14 us (3%)
  local copies, waits for them, and re-layouts  5.14 us (3%)
    reduce_scatter x1, waiting for transfers between devices, on_device(): lax.psum_scatter(blocked, 'shard', scatter_dimension=0, tiled=True)  67.2 us
    reduce_scatter x1, waiting for transfers between devices, on_device(): lax.psum_scatter(lax.dot_general(tokens_in, cotangent, (((0,), (0,)), (()...  47.3 us
    all_gather x1, waiting for transfers between devices, on_device(): lax.all_gather(group_rows, 'shard', axis=0, tiled=True)  44.9 us
    all_gather x1, blocking collectives, on_device(): group_rows = lax.all_gather(low_weight, 'replica', axis=0, tiled=True)  6.22 us
  transfers between devices with their start and end apart: 3, of which 3 were waited for; matrix products, arithmetic and copies ran while one was open for 2% of the time, Pallas kernels for 0%

commit v1 on v0

v1 whole, which is shorter than its diff:
```python
import functools

import jax
import jax.numpy as jnp
from jax import lax
from jax.experimental import pallas as pl
from jax.experimental.pallas import tpu as pltpu
from jax.sharding import PartitionSpec as P

beta_one = 0.9
beta_two = 0.95
learn_rate = 0.003
decay_rate = 0.1
epsilon = 1e-08
steps_done = 10

MESH = pl.DeviceIdType.MESH
PAIR = 2


def adam(gradient, master, first_moment, second_moment):
    new_first = beta_one * first_moment + (1.0 - beta_one) * gradient
    new_second = beta_two * second_moment + (1.0 - beta_two) * gradient * gradient
    first_hat = new_first / (1.0 - beta_one**steps_done)
    second_hat = new_second / (1.0 - beta_two**steps_done)
    new_master = master - learn_rate * (
        first_hat / (jnp.sqrt(second_hat) + epsilon) + decay_rate * master
    )
    return new_master, new_first, new_second


def kernel(
    Z, own,
    tok_hbm, cot_hbm, nxt_hbm, master_hbm, first_hbm, second_hbm,
    nm_hbm, nf_hbm, ns_hbm, out_ref,
    tok, cot, nxt, state, fresh,
    g32, gb, rc, hb, rp, jb, rq, kb, rz, wall, acc, ro,
    tok_sem, cot_sem, nxt_sem, state_sem, fresh_sem,
    swap_s, swap_r, c_s, c_r, p_s, p_r, q_s, q_r, z_s, z_r,
    az_s, az_r, aq_s, aq_r, ap_s, ap_r, o_s, o_r,
):
    f32, bf16 = jnp.float32, jnp.bfloat16
    r, s = lax.axis_index("replica"), lax.axis_index("shard")
    y, c, z, x = r // PAIR, r % PAIR, s // PAIR, s % PAIR
    p, q = x * (1 - c) + y * c, y * (1 - c) + x * c
    wide = PAIR * own
    half_cols = Z * wide

    def at(yy, cc, zz, xx):
        return (yy * PAIR + cc, zz * PAIR + xx)

    sib = at(y, 1 - c, z, x)
    p_peer = at(y * (1 - c) + (1 - y) * c, c, z, (1 - x) * (1 - c) + x * c)
    q_peer = at((1 - y) * (1 - c) + y * c, c, z, x * (1 - c) + (1 - x) * c)

    def z_at(j):
        return at(y, c, (z + j) % Z, x)

    loads = []
    cot_load = pltpu.make_async_copy(cot_hbm, cot, cot_sem)
    cot_load.start()
    for k in range(Z):
        zc = (z + 1 + k) % Z
        row = []
        for yc in range(PAIR * PAIR):
            col = pl.multiple_of((yc * Z + zc) * wide, own)
            cp = pltpu.make_async_copy(
                tok_hbm.at[:, pl.ds(col, wide)], tok.at[k, yc], tok_sem.at[k, yc]
            )
            cp.start()
            row.append(cp)
        loads.append(row)

    barrier = pltpu.get_barrier_semaphore()
    peers = [sib, p_peer, q_peer] + [z_at(j) for j in range(1, Z)]
    for d in peers:
        pl.semaphore_signal(barrier, inc=1, device_id=d, device_id_type=MESH)

    state_loads = [
        pltpu.make_async_copy(src, state.at[i], state_sem.at[i])
        for i, src in enumerate((master_hbm, first_hbm, second_hbm))
    ]
    rows = nxt_hbm.shape[0]
    nxt_loads = []
    for yy in range(PAIR):
        col = pl.multiple_of((yy * PAIR + c) * half_cols, own)
        nxt_loads.append(
            pltpu.make_async_copy(
                nxt_hbm.at[:, pl.ds(col, half_cols)], nxt.at[yy, pl.ds(0, rows)], nxt_sem.at[yy]
            )
        )
    for cp in state_loads + nxt_loads:
        cp.start()

    def send(src, dst, s_sem, r_sem, dev):
        cp = pltpu.make_async_remote_copy(
            src_ref=src, dst_ref=dst, send_sem=s_sem, recv_sem=r_sem,
            device_id=dev, device_id_type=MESH,
        )
        cp.start()
        return cp

    sent = []
    cot_load.wait()
    cot_t = cot[...].astype(f32).T.astype(bf16)
    core_cp, p_cp, q_cp, z_cp, swaps = {}, {}, {}, {}, []

    def compute(k):
        for cp in loads[k]:
            cp.wait()
        for yy in range(PAIR):
            for h in range(PAIR):
                for xx in range(PAIR):
                    pp, qq = (xx, yy) if h == 0 else (yy, xx)
                    block = jnp.dot(
                        cot_t, tok[k, yy * PAIR + h, :, xx * own:(xx + 1) * own],
                        preferred_element_type=f32,
                    )
                    g32[k, h, pp, qq] = block
                    gb[k, h, pp, qq] = block.astype(bf16)

    def stage_core(k):
        core_cp[k] = send(gb.at[k, 1 - c], rc.at[k], c_s.at[k], c_r.at[k], sib)

    def stage_p(k):
        core_cp[k].wait_recv()
        for qq in range(PAIR):
            hb[k, qq] = (g32[k, c, 1 - p, qq] + rc[k, 1 - p, qq].astype(f32)).astype(bf16)
        p_cp[k] = send(hb.at[k], rp.at[k], p_s.at[k], p_r.at[k], p_peer)

    def partial(k, qq):
        return g32[k, c, p, qq] + rc[k, p, qq].astype(f32) + rp[k, qq].astype(f32)

    def stage_q(k):
        p_cp[k].wait_recv()
        jb[k] = partial(k, 1 - q).astype(bf16)
        q_cp[k] = send(jb.at[k], rq.at[k], q_s.at[k], q_r.at[k], q_peer)

    def stage_z(k):
        q_cp[k].wait_recv()
        total = partial(k, q) + rq[k].astype(f32)
        if k == Z - 1:
            return total
        kb[k] = total.astype(bf16)
        z_cp[k] = send(kb.at[k], rz.at[k], z_s.at[k], z_r.at[k], z_at(k + 1))
        return None

    total = None
    for t in range(Z + 3):
        if t < Z:
            compute(t)
            if t == 0:
                pl.semaphore_wait(barrier, len(peers))
            stage_core(t)
            if t == Z - 1:
                for yy in range(PAIR):
                    col = pl.multiple_of((yy * PAIR + 1 - c) * half_cols, own)
                    swaps.append(
                        send(
                            nxt_hbm.at[:, pl.ds(col, half_cols)], nxt.at[yy, pl.ds(rows, rows)],
                            swap_s.at[yy], swap_r.at[yy], sib,
                        )
                    )
        if 0 <= t - 1 < Z:
            stage_p(t - 1)
        if 0 <= t - 2 < Z:
            stage_q(t - 2)
        if 0 <= t - 3 < Z:
            total = stage_z(t - 3)

    for k in range(Z - 1):
        z_cp[k].wait_recv()
        total = total + rz[k].astype(f32)
    for cp in state_loads:
        cp.wait()
    new_master, new_first, new_second = adam(total.T, state[0], state[1], state[2])
    wall[z, p, q] = new_master.astype(bf16)

    az, aq, ap = {}, {}, {}
    for j in range(1, Z):
        az[j] = send(
            wall.at[z, p, q], wall.at[z, p, q], az_s.at[j - 1], az_r.at[j - 1], z_at(j)
        )

    def forward(j):
        zj = (z - j + Z) % Z
        aq[j] = send(wall.at[zj, p, q], wall.at[zj, p, q], aq_s.at[j], aq_r.at[j], q_peer)
        ap[j, 0] = send(
            wall.at[zj, p, q], wall.at[zj, p, q], ap_s.at[j, 0], ap_r.at[j, 0], p_peer
        )

    def forward_second(j):
        zj = (z - j + Z) % Z
        aq[j].wait_recv()
        ap[j, 1] = send(
            wall.at[zj, p, 1 - q], wall.at[zj, p, 1 - q], ap_s.at[j, 1], ap_r.at[j, 1], p_peer
        )

    def product(j, pp, qq):
        zj = (z - j + Z) % Z
        yy, xx = qq * (1 - c) + pp * c, pp * (1 - c) + qq * c
        col = pl.multiple_of((zj * PAIR + xx) * own, own)
        return jnp.dot(
            nxt[yy, :, pl.ds(col, own)], wall[zj, pp, qq], preferred_element_type=f32
        )

    forward(0)
    for i, value in enumerate((new_master, new_first, new_second)):
        fresh[i] = value
    stores = [
        pltpu.make_async_copy(fresh.at[i], dst, fresh_sem.at[i])
        for i, dst in enumerate((nm_hbm, nf_hbm, ns_hbm))
    ]
    for cp in stores:
        cp.start()
    for cp in nxt_loads:
        cp.wait()
    for cp in swaps:
        cp.wait_recv()
    acc[...] = product(0, p, q)
    for j in range(1, Z):
        az[j].wait_recv()
        forward(j)
        forward_second(j - 1)
        acc[...] += product(j, p, q) + product(j - 1, p, 1 - q)
        ap[j - 1, 0].wait_recv()
        acc[...] += product(j - 1, 1 - p, q)
    forward_second(Z - 1)
    acc[...] += product(Z - 1, p, 1 - q)
    for j in range(Z - 1):
        ap[j, 1].wait_recv()
        acc[...] += product(j, 1 - p, 1 - q)
    ap[Z - 1, 0].wait_recv()
    acc[...] += product(Z - 1, 1 - p, q)
    ap[Z - 1, 1].wait_recv()
    acc[...] += product(Z - 1, 1 - p, 1 - q)

    last = send(acc.at[pl.ds(rows, rows)], ro, o_s, o_r, sib)
    for cps in (core_cp, p_cp, q_cp, z_cp, az, aq, ap):
        for cp in cps.values():
            cp.wait_send()
    for cp in swaps:
        cp.wait_send()
    for cp in stores:
        cp.wait()
    last.wait_recv()
    out_ref[...] = (acc[pl.ds(0, rows)] + ro[...]).astype(bf16)
    last.wait_send()


def fused(Z, tokens_in, cotangent, next_tokens, master, first_moment, second_moment):
    f32, bf16 = jnp.float32, jnp.bfloat16
    own, cols = master.shape
    count = tokens_in.shape[0]
    rows = next_tokens.shape[0]
    dma = pltpu.SemaphoreType.DMA
    block = (cols, own)
    any_spec = pl.BlockSpec(memory_space=pl.ANY)
    scratch = [
        pltpu.VMEM((Z, PAIR * PAIR, count, PAIR * own), bf16),
        pltpu.VMEM((count, cols), bf16),
        pltpu.VMEM((PAIR, 2 * rows, Z * PAIR * own), bf16),
        pltpu.VMEM((3, own, cols), f32),
        pltpu.VMEM((3, own, cols), f32),
        pltpu.VMEM((Z, PAIR, PAIR, PAIR) + block, f32),
        pltpu.VMEM((Z, PAIR, PAIR, PAIR) + block, bf16),
        pltpu.VMEM((Z, PAIR, PAIR) + block, bf16),
        pltpu.VMEM((Z, PAIR) + block, bf16),
        pltpu.VMEM((Z, PAIR) + block, bf16),
        pltpu.VMEM((Z,) + block, bf16),
        pltpu.VMEM((Z,) + block, bf16),
        pltpu.VMEM((Z - 1,) + block, bf16),
        pltpu.VMEM((Z - 1,) + block, bf16),
        pltpu.VMEM((Z, PAIR, PAIR, own, cols), bf16),
        pltpu.VMEM((2 * rows, cols), f32),
        pltpu.VMEM((rows, cols), f32),
        dma((Z, PAIR * PAIR)), dma, dma((PAIR,)), dma((3,)), dma((3,)),
        dma((PAIR,)), dma((PAIR,)),
        dma((Z,)), dma((Z,)), dma((Z,)), dma((Z,)), dma((Z,)), dma((Z,)),
        dma((Z - 1,)), dma((Z - 1,)),
        dma((Z - 1,)), dma((Z - 1,)), dma((Z,)), dma((Z,)), dma((Z, 2)), dma((Z, 2)),
        dma, dma,
    ]
    return pl.pallas_call(
        functools.partial(kernel, Z, own),
        out_shape=(
            jax.ShapeDtypeStruct(master.shape, f32),
            jax.ShapeDtypeStruct(master.shape, f32),
            jax.ShapeDtypeStruct(master.shape, f32),
            jax.ShapeDtypeStruct((rows, cols), bf16),
        ),
        in_specs=[any_spec] * 6,
        out_specs=(any_spec, any_spec, any_spec, pl.BlockSpec(memory_space=pltpu.VMEM)),
        scratch_shapes=scratch,
        compiler_params=pltpu.CompilerParams(
            collective_id=0, has_side_effects=True, vmem_limit_bytes=32 * 2**20
        ),
    )(tokens_in, cotangent, next_tokens, master, first_moment, second_moment)


def plain(tokens_in, cotangent, next_tokens, master, first_moment, second_moment):
    n_rep = lax.axis_size("replica")
    n_shard = lax.axis_size("shard")
    model_width = tokens_in.shape[1]
    own_rows = model_width // (n_rep * n_shard)
    blocked = lax.psum_scatter(
        lax.dot_general(
            tokens_in, cotangent, (((0,), (0,)), ((), ())), preferred_element_type=jnp.float32
        ),
        "replica",
        scatter_dimension=0,
        tiled=True,
    )
    gradient = lax.psum_scatter(blocked, "shard", scatter_dimension=0, tiled=True)
    new_master, new_first, new_second = adam(gradient, master, first_moment, second_moment)
    low_weight = new_master.astype(jnp.bfloat16)
    group_rows = lax.all_gather(low_weight, "replica", axis=0, tiled=True)
    row_count = next_tokens.shape[0]
    arranged = next_tokens.reshape(row_count, n_rep, n_shard, own_rows).transpose(0, 2, 1, 3)
    columns = arranged.reshape(row_count, model_width)
    summed = jnp.dot(
        columns,
        lax.all_gather(group_rows, "shard", axis=0, tiled=True),
        preferred_element_type=jnp.float32,
    )
    return (new_master, new_first, new_second, summed.astype(jnp.bfloat16))


def solution(mesh):
    n_rep, n_shard = mesh.shape["replica"], mesh.shape["shard"]

    def on_device(tokens_in, cotangent, next_tokens, master, first_moment, second_moment):
        own, cols = master.shape
        fits = (
            n_rep == PAIR * PAIR
            and n_shard % PAIR == 0
            and n_shard > PAIR
            and own % 128 == 0
            and cols % 128 == 0
            and next_tokens.shape[0] % 16 == 0
            and tokens_in.shape[0] % 128 == 0
        )
        args = (tokens_in, cotangent, next_tokens, master, first_moment, second_moment)
        if fits:
            return tuple(fused(n_shard // PAIR, *args))
        return plain(*args)

    spec = P(("replica", "shard"), None)
    return jax.shard_map(
        on_device, mesh=mesh, in_specs=(spec,) * 6, out_specs=(spec,) * 4, check_vma=False
    )
```

time: 193 us -> 49.9 us (0.26)
  waiting for transfers between devices: 159 us -> 0 us
  Pallas kernels: 0 us -> 40.1 us
  between operations: 13.8 us -> 0.66 us
  blocking collectives: 6.22 us -> 0 us
  matrix products: 6.14 us -> 0 us
  local copies, waits for them, and re-layouts: 5.14 us -> 8.85 us
    reduce_scatter x2 -> x0, waiting for transfers between devices: 115 us -> none  [the longest x1 67.2 us: on_device(): lax.psum_scatter(blocked, 'shard', scatter_dimension=0, tiled=True)]
    all_gather x1 -> x0, waiting for transfers between devices: 44.9 us -> none  [on_device(): lax.all_gather(group_rows, 'shard', axis=0, tiled=True)]
    pallas_call x0 -> x1, Pallas kernels: none -> 40.1 us  [fused(): pl.pallas_call(functools.partial(kernel, Z, own), out_shape=(jax.ShapeDty...]
    unnamed x11 -> x16, local copies, waits for them, and re-layouts: 1.82 us -> 8.85 us
    all_gather x1 -> x0, blocking collectives: 6.22 us -> none  [on_device(): group_rows = lax.all_gather(low_weight, 'replica', axis=0, tiled=True)]
    dot_general x2 -> x0, matrix products: 6.14 us -> none  [the longest x1 3.45 us: on_device(): lax.dot_general(tokens_in, cotangent, (((0,), (0,)), ((), ())), preferred...]
    reshape x2 -> x0, local copies, waits for them, and re-layouts: 3.33 us -> none  [the longest x1 1.81 us: on_device(): columns = arranged.reshape(row_count, model_width)]
  transfers between devices with their start and end apart: 3 -> 0, of which waited for: 3 -> 0; matrix products, arithmetic and copies ran while one was open for 2% -> 0% of each run, Pallas kernels for 0% -> 0%
where the time goes in v1:
time: 49.9 us; the launch traced here: 49.6 us
  Pallas kernels  40.1 us (80%)
  local copies, waits for them, and re-layouts  8.85 us (18%)
  between operations  0.66 us (1%)
    pallas_call x1, Pallas kernels, fused(): pl.pallas_call(functools.partial(kernel, Z, own), out_shape=(jax.ShapeDty...  40.1 us
    unnamed x16, local copies, waits for them, and re-layouts  8.85 us

profile of v1, /device:TPU:0, one launch (start us, length us, event | category | flops | bytes accessed | tf_op | source)
XLA Modules:
  0.0 49.6 jit_solution(7165609938353839042)
XLA Ops:
  0.6 0.0 copy-start
  0.6 1.6 %copy-done = bf16[128,8192]{1,0:T(8,128)(2,1)S(1)} copy-done((bf16[128,8192]{1,0:T(8,128)(2,1)S(1)}, bf16[128,8192]{1,0:T(8,128)(2,1)}, u32[]{:S(2)}) %copy-start) | copy-done | bytes 2097176
  2.2 0.0 copy-start.1
  2.2 1.2 %copy-done.1 = bf16[64,8192]{1,0:T(8,128)(2,1)S(1)} copy-done((bf16[64,8192]{1,0:T(8,128)(2,1)S(1)}, bf16[64,8192]{1,0:T(8,128)(2,1)}, u32[]{:S(2)}) %copy-start.1) | copy-done | bytes 1048600
  3.5 0.0 copy-start.2
  3.5 0.9 %copy-done.2 = f32[256,128]{1,0:T(8,128)S(1)} copy-done((f32[256,128]{1,0:T(8,128)S(1)}, f32[256,128]{1,0:T(8,128)}, u32[]{:S(2)}) %copy-start.2) | copy-done | bytes 131096
  4.4 0.0 copy-start.3
  4.4 0.9 %copy-done.3 = f32[256,128]{1,0:T(8,128)S(1)} copy-done((f32[256,128]{1,0:T(8,128)S(1)}, f32[256,128]{1,0:T(8,128)}, u32[]{:S(2)}) %copy-start.3) | copy-done | bytes 131096
  5.3 0.0 copy-start.4
  5.3 0.9 %copy-done.4 = f32[256,128]{1,0:T(8,128)S(1)} copy-done((f32[256,128]{1,0:T(8,128)S(1)}, f32[256,128]{1,0:T(8,128)}, u32[]{:S(2)}) %copy-start.4) | copy-done | bytes 131096
  6.2 0.0 copy-start.5
  6.2 0.8 %copy-done.5 = bf16[128,128]{1,0:T(8,128)(2,1)S(1)} copy-done((bf16[128,128]{1,0:T(8,128)(2,1)S(1)}, bf16[128,128]{1,0:T(8,128)(2,1)}, u32[]{:S(2)}) %copy-start.5) | copy-done | bytes 32792
  6.9 40.1 %shard_map.93 = (f32[256,128]{1,0:T(8,128)S(1)}, f32[256,128]{1,0:T(8,128)S(1)}, f32[256,128]{1,0:T(8,128)S(1)}, bf16[64,128]{1,0:T(8,128)(2,1)S(1)}) custom-call(bf16[128,8192]{1,0:T(8,128)(2,1)S(1)} %copy-done, bf16[128,128]{1,0:T(8,128)(2,1)S(1)} %copy-done.5, bf16[64,8192]{1,0:T(8,128)(2,1)S(1)} %copy-done.1, f32[256,128]{1,0:T(8,128)S(1)} %copy-done.2, ...), custom_call_target="tpu_custom_call" | custom-call | tf_op jit(solution)/shard_map/pallas_call | solution.py:284
  47.0 0.7 %copy.14 = f32[256,128]{1,0:T(8,128)} copy(f32[256,128]{1,0:T(8,128)S(1)} %get-tuple-element.8) | data formatting | bytes 262144
  47.7 0.7 %copy.15 = f32[256,128]{1,0:T(8,128)} copy(f32[256,128]{1,0:T(8,128)S(1)} %get-tuple-element.9) | data formatting | bytes 262144
  48.3 0.7 %copy.16 = f32[256,128]{1,0:T(8,128)} copy(f32[256,128]{1,0:T(8,128)S(1)} %get-tuple-element.10) | data formatting | bytes 262144
  49.0 0.6 %copy.17 = bf16[64,128]{1,0:T(8,128)(2,1)} copy(bf16[64,128]{1,0:T(8,128)(2,1)S(1)} %get-tuple-element.11) | data formatting | bytes 32768
Async XLA Ops:
  0.6 1.6 %copy-start = (bf16[128,8192]{1,0:T(8,128)(2,1)S(1)}, bf16[128,8192]{1,0:T(8,128)(2,1)}, u32[]{:S(2)}) copy-start(bf16[128,8192]{1,0:T(8,128)(2,1)} %tok_hbm.1) | copy-start | bytes 6291460
  2.2 1.2 %copy-start.1 = (bf16[64,8192]{1,0:T(8,128)(2,1)S(1)}, bf16[64,8192]{1,0:T(8,128)(2,1)}, u32[]{:S(2)}) copy-start(bf16[64,8192]{1,0:T(8,128)(2,1)} %nxt_hbm.1) | copy-start | bytes 3145732
  3.5 0.9 %copy-start.2 = (f32[256,128]{1,0:T(8,128)S(1)}, f32[256,128]{1,0:T(8,128)}, u32[]{:S(2)}) copy-start(f32[256,128]{1,0:T(8,128)} %master_hbm.1) | copy-start | bytes 393220
  4.4 0.9 %copy-start.3 = (f32[256,128]{1,0:T(8,128)S(1)}, f32[256,128]{1,0:T(8,128)}, u32[]{:S(2)}) copy-start(f32[256,128]{1,0:T(8,128)} %first_hbm.1) | copy-start | bytes 393220
  5.3 0.9 %copy-start.4 = (f32[256,128]{1,0:T(8,128)S(1)}, f32[256,128]{1,0:T(8,128)}, u32[]{:S(2)}) copy-start(f32[256,128]{1,0:T(8,128)} %second_hbm.1) | copy-start | bytes 393220
  6.2 0.8 %copy-start.5 = (bf16[128,128]{1,0:T(8,128)(2,1)S(1)}, bf16[128,128]{1,0:T(8,128)(2,1)}, u32[]{:S(2)}) copy-start(bf16[128,128]{1,0:T(8,128)(2,1)} %cot_hbm.1) | copy-start | bytes 98308

commit v2 on v1

v2 whole, which is shorter than its diff:
```python
import functools

import jax
import jax.numpy as jnp
from jax import lax
from jax.experimental import pallas as pl
from jax.experimental.pallas import tpu as pltpu
from jax.sharding import PartitionSpec as P

beta_one = 0.9
beta_two = 0.95
learn_rate = 0.003
decay_rate = 0.1
epsilon = 1e-08
steps_done = 10

MESH = pl.DeviceIdType.MESH
PAIR = 2
VMEM_BYTES = 62 * 2**20


def adam(gradient, master, first_moment, second_moment):
    new_first = beta_one * first_moment + (1.0 - beta_one) * gradient
    new_second = beta_two * second_moment + (1.0 - beta_two) * gradient * gradient
    first_hat = new_first / (1.0 - beta_one**steps_done)
    second_hat = new_second / (1.0 - beta_two**steps_done)
    new_master = master - learn_rate * (
        first_hat / (jnp.sqrt(second_hat) + epsilon) + decay_rate * master
    )
    return new_master, new_first, new_second


def kernel(
    Z, own,
    tok_hbm, cot_hbm, nxt_hbm, master_hbm, first_hbm, second_hbm,
    nm_out, nf_out, ns_out, out_ref,
    tok, cot, nxt, state, fresh,
    g32, gb, rc, hb, rp, jb, rq, kb, rz, wall, acc, ro,
    tok_sem, cot_sem, nxt_sem, state_sem, fresh_sem,
    n_s, n_r, c_s, c_r, p_s, p_r, q_s, q_r, z_s, z_r,
    az_s, az_r, aq_s, aq_r, o_s, o_r,
):
    f32, bf16 = jnp.float32, jnp.bfloat16
    r, s = lax.axis_index("replica"), lax.axis_index("shard")
    y, c, z, x = r // PAIR, r % PAIR, s // PAIR, s % PAIR
    p, q = x * (1 - c) + y * c, y * (1 - c) + x * c
    wide = PAIR * own
    rows = nxt_hbm.shape[0]

    def at(yy, cc, zz, xx):
        return (yy * PAIR + cc, zz * PAIR + xx)

    def over_p(cc):
        return at(y * (1 - c) + (1 - y) * c, cc, z, (1 - x) * (1 - c) + x * c)

    def over_q(cc):
        return at((1 - y) * (1 - c) + y * c, cc, z, x * (1 - c) + (1 - x) * c)

    def z_at(j):
        return at(y, c, (z + j) % Z, x)

    def block_at(h, pp, qq, zz):
        yy, xx = qq * (1 - h) + pp * h, pp * (1 - h) + qq * h
        return ((yy * PAIR + h) * Z + zz) * PAIR + xx

    sib, p_peer, q_peer = at(y, 1 - c, z, x), over_p(c), over_q(c)

    loads = []
    cot_load = pltpu.make_async_copy(cot_hbm, cot, cot_sem)
    cot_load.start()
    for k in range(Z):
        zc = (z + 1 + k) % Z
        row = []
        for yc in range(PAIR * PAIR):
            col = pl.multiple_of((yc * Z + zc) * wide, own)
            cp = pltpu.make_async_copy(
                tok_hbm.at[:, pl.ds(col, wide)], tok.at[k, yc], tok_sem.at[k, yc]
            )
            cp.start()
            row.append(cp)
        loads.append(row)
        if k == 0:
            barrier = pltpu.get_barrier_semaphore()
            peers = [sib, p_peer, q_peer, over_p(1 - c), over_q(1 - c)]
            peers += [z_at(j) for j in range(1, Z)]
            for d in peers:
                pl.semaphore_signal(barrier, inc=1, device_id=d, device_id_type=MESH)

    def send(src, dst, s_sem, r_sem, dev):
        cp = pltpu.make_async_remote_copy(
            src_ref=src, dst_ref=dst, send_sem=s_sem, recv_sem=r_sem,
            device_id=dev, device_id_type=MESH,
        )
        cp.start()
        return cp

    cot_load.wait()
    cot_t = cot[...].astype(f32).T.astype(bf16)
    core_cp, p_cp, q_cp, z_cp = {}, {}, {}, {}

    def term(k, h, yy, xx):
        return jnp.dot(
            cot_t, tok[k, yy * PAIR + h, :, xx * own:(xx + 1) * own],
            preferred_element_type=f32,
        )

    def place(h, yy, xx):
        return xx * (1 - h) + yy * h, yy * (1 - h) + xx * h

    def stage_core(k):
        for cp in loads[k]:
            cp.wait()
        for yy in range(PAIR):
            for xx in range(PAIR):
                gb[(k,) + place(1 - c, yy, xx)] = term(k, 1 - c, yy, xx).astype(bf16)
        if k == 0:
            pl.semaphore_wait(barrier, len(peers))
        core_cp[k] = send(gb.at[k], rc.at[k], c_s.at[k], c_r.at[k], sib)

    def own_terms(k):
        for yy in range(PAIR):
            for xx in range(PAIR):
                g32[(k,) + place(c, yy, xx)] = term(k, c, yy, xx)

    def stage_p(k):
        core_cp[k].wait_recv()
        for qq in range(PAIR):
            hb[k, qq] = (g32[k, 1 - p, qq] + rc[k, 1 - p, qq].astype(f32)).astype(bf16)
        p_cp[k] = send(hb.at[k], rp.at[k], p_s.at[k], p_r.at[k], p_peer)

    def partial(k, qq):
        return g32[k, p, qq] + rc[k, p, qq].astype(f32) + rp[k, qq].astype(f32)

    def stage_q(k):
        p_cp[k].wait_recv()
        jb[k] = partial(k, 1 - q).astype(bf16)
        q_cp[k] = send(jb.at[k], rq.at[k], q_s.at[k], q_r.at[k], q_peer)

    def stage_z(k):
        q_cp[k].wait_recv()
        total = partial(k, q) + rq[k].astype(f32)
        if k == Z - 1:
            return total
        kb[k] = total.astype(bf16)
        z_cp[k] = send(kb.at[k], rz.at[k], z_s.at[k], z_r.at[k], z_at(k + 1))
        return None

    swaps, nxt_loads = {}, {}

    def swap(i, who):
        h, pp, qq, dev = (
            (1 - c, q, p, sib), (c, 1 - p, q, p_peer), (1 - c, 1 - q, p, over_q(1 - c))
        )[who]
        qq = qq if i == 0 else 1 - qq
        for j in range(Z):
            zj = (z - j + Z) % Z
            col = pl.multiple_of(block_at(h, pp, qq, zj) * own, own)
            swaps[i, who, j] = send(
                nxt_hbm.at[:, pl.ds(col, own)], nxt.at[zj, qq, pl.ds((who + 1) * rows, rows)],
                n_s.at[i, who, j], n_r.at[i, who, j], dev,
            )

    def local_tokens():
        for i in range(PAIR):
            qq = q if i == 0 else 1 - q
            for j in range(Z):
                zj = (z - j + Z) % Z
                col = pl.multiple_of(block_at(c, p, qq, zj) * own, own)
                cp = pltpu.make_async_copy(
                    nxt_hbm.at[:, pl.ds(col, own)], nxt.at[zj, qq, pl.ds(0, rows)], nxt_sem.at[i, j]
                )
                cp.start()
                nxt_loads[i, j] = cp

    state_loads = [
        pltpu.make_async_copy(src, state.at[i], state_sem.at[i])
        for i, src in enumerate((master_hbm, first_hbm, second_hbm))
    ]
    total = None
    for t in range(Z + 3):
        if t < Z:
            stage_core(t)
            if t == 0:
                swap(0, 1)
                swap(0, 2)
            own_terms(t)
        if 0 <= t - 1 < Z:
            stage_p(t - 1)
        if t == Z:
            swap(0, 0)
            swap(1, 0)
            local_tokens()
            for cp in state_loads:
                cp.start()
        if 0 <= t - 2 < Z:
            stage_q(t - 2)
        if t == Z + 1:
            swap(1, 1)
            swap(1, 2)
        if 0 <= t - 3 < Z:
            total = stage_z(t - 3)

    for cp in state_loads:
        cp.wait()
    for k in range(Z - 1):
        z_cp[k].wait_recv()
        total = total + rz[k].astype(f32)
    new_master, new_first, new_second = adam(total.T, state[0], state[1], state[2])
    wall[z, q] = new_master.astype(bf16)

    az, aq = {}, {}
    for j in range(1, Z):
        az[j] = send(wall.at[z, q], wall.at[z, q], az_s.at[j - 1], az_r.at[j - 1], z_at(j))

    def forward(j):
        zj = (z - j + Z) % Z
        aq[j] = send(wall.at[zj, q], wall.at[zj, q], aq_s.at[j], aq_r.at[j], q_peer)

    def product(j, i):
        zj = (z - j + Z) % Z
        qq = q if i == 0 else 1 - q
        nxt_loads[i, j].wait()
        for who in range(3):
            swaps[i, who, j].wait_recv()
        return jnp.dot(nxt[zj, qq], wall[zj, qq], preferred_element_type=f32)

    forward(0)
    for i, value in enumerate((new_master, new_first, new_second)):
        fresh[i] = value
    stores = [
        pltpu.make_async_copy(fresh.at[i], dst, fresh_sem.at[i])
        for i, dst in enumerate((nm_out, nf_out, ns_out))
    ]
    for cp in stores:
        cp.start()
    acc[...] = product(0, 0)
    for j in range(1, Z):
        az[j].wait_recv()
        forward(j)
        acc[...] += product(j, 0)
        aq[j - 1].wait_recv()
        acc[...] += product(j - 1, 1)
    aq[Z - 1].wait_recv()
    acc[...] += product(Z - 1, 1)

    last = [
        send(acc.at[pl.ds((who + 1) * rows, rows)], ro.at[who], o_s.at[who], o_r.at[who], dev)
        for who, dev in ((1, p_peer), (2, over_p(1 - c)), (0, sib))
    ]
    for cps in (core_cp, p_cp, q_cp, z_cp, az, aq, swaps):
        for cp in cps.values():
            cp.wait_send()
    for cp in stores:
        cp.wait()
    for cp in last:
        cp.wait_recv()
    out_ref[...] = (acc[pl.ds(0, rows)] + ro[0] + ro[1] + ro[2]).astype(bf16)
    for cp in last:
        cp.wait_send()


def write_out(a, b, c, d, a_out, b_out, c_out, d_out, sem):
    copies = [
        pltpu.make_async_copy(src, dst, sem.at[i])
        for i, (src, dst) in enumerate(((a, a_out), (b, b_out), (c, c_out), (d, d_out)))
    ]
    for cp in copies:
        cp.start()
    for cp in copies:
        cp.wait()


def fused(Z, tokens_in, cotangent, next_tokens, master, first_moment, second_moment):
    f32, bf16 = jnp.float32, jnp.bfloat16
    own, cols = master.shape
    count = tokens_in.shape[0]
    rows = next_tokens.shape[0]
    dma = pltpu.SemaphoreType.DMA
    block = (cols, own)
    any_spec = pl.BlockSpec(memory_space=pl.ANY)
    hbm_spec = pl.BlockSpec(memory_space=pltpu.HBM)
    scratch = [
        pltpu.VMEM((Z, PAIR * PAIR, count, PAIR * own), bf16),
        pltpu.VMEM((count, cols), bf16),
        pltpu.VMEM((Z, PAIR, 4 * rows, own), bf16),
        pltpu.VMEM((3, own, cols), f32),
        pltpu.VMEM((3, own, cols), f32),
        pltpu.VMEM((Z, PAIR, PAIR) + block, f32),
        pltpu.VMEM((Z, PAIR, PAIR) + block, bf16),
        pltpu.VMEM((Z, PAIR, PAIR) + block, bf16),
        pltpu.VMEM((Z, PAIR) + block, bf16),
        pltpu.VMEM((Z, PAIR) + block, bf16),
        pltpu.VMEM((Z,) + block, bf16),
        pltpu.VMEM((Z,) + block, bf16),
        pltpu.VMEM((Z - 1,) + block, bf16),
        pltpu.VMEM((Z - 1,) + block, bf16),
        pltpu.VMEM((Z, PAIR, own, cols), bf16),
        pltpu.VMEM((4 * rows, cols), f32),
        pltpu.VMEM((3, rows, cols), f32),
        dma((Z, PAIR * PAIR)), dma, dma((PAIR, Z)), dma((3,)), dma((3,)),
        dma((PAIR, 3, Z)), dma((PAIR, 3, Z)),
        dma((Z,)), dma((Z,)), dma((Z,)), dma((Z,)), dma((Z,)), dma((Z,)),
        dma((Z - 1,)), dma((Z - 1,)),
        dma((Z - 1,)), dma((Z - 1,)), dma((Z,)), dma((Z,)), dma((3,)), dma((3,)),
    ]
    out_shape = (
        jax.ShapeDtypeStruct(master.shape, f32),
        jax.ShapeDtypeStruct(master.shape, f32),
        jax.ShapeDtypeStruct(master.shape, f32),
        jax.ShapeDtypeStruct((rows, cols), bf16),
    )
    results = pl.pallas_call(
        functools.partial(kernel, Z, own),
        out_shape=out_shape,
        in_specs=[hbm_spec] * 6,
        out_specs=(any_spec, any_spec, any_spec, pl.BlockSpec(memory_space=pltpu.VMEM)),
        scratch_shapes=scratch,
        compiler_params=pltpu.CompilerParams(
            collective_id=0, has_side_effects=True, vmem_limit_bytes=VMEM_BYTES
        ),
    )(tokens_in, cotangent, next_tokens, master, first_moment, second_moment)
    return pl.pallas_call(
        write_out,
        out_shape=out_shape,
        in_specs=[any_spec] * 4,
        out_specs=(hbm_spec,) * 4,
        scratch_shapes=[dma((4,))],
        compiler_params=pltpu.CompilerParams(vmem_limit_bytes=VMEM_BYTES),
    )(*results)


def plain(tokens_in, cotangent, next_tokens, master, first_moment, second_moment):
    n_rep = lax.axis_size("replica")
    n_shard = lax.axis_size("shard")
    model_width = tokens_in.shape[1]
    own_rows = model_width // (n_rep * n_shard)
    blocked = lax.psum_scatter(
        lax.dot_general(
            tokens_in, cotangent, (((0,), (0,)), ((), ())), preferred_element_type=jnp.float32
        ),
        "replica",
        scatter_dimension=0,
        tiled=True,
    )
    gradient = lax.psum_scatter(blocked, "shard", scatter_dimension=0, tiled=True)
    new_master, new_first, new_second = adam(gradient, master, first_moment, second_moment)
    low_weight = new_master.astype(jnp.bfloat16)
    group_rows = lax.all_gather(low_weight, "replica", axis=0, tiled=True)
    row_count = next_tokens.shape[0]
    arranged = next_tokens.reshape(row_count, n_rep, n_shard, own_rows).transpose(0, 2, 1, 3)
    columns = arranged.reshape(row_count, model_width)
    summed = jnp.dot(
        columns,
        lax.all_gather(group_rows, "shard", axis=0, tiled=True),
        preferred_element_type=jnp.float32,
    )
    return (new_master, new_first, new_second, summed.astype(jnp.bfloat16))


def solution(mesh):
    n_rep, n_shard = mesh.shape["replica"], mesh.shape["shard"]

    def on_device(tokens_in, cotangent, next_tokens, master, first_moment, second_moment):
        own, cols = master.shape
        fits = (
            n_rep == PAIR * PAIR
            and n_shard % PAIR == 0
            and n_shard > PAIR
            and own % 128 == 0
            and cols % 128 == 0
            and next_tokens.shape[0] % 16 == 0
            and tokens_in.shape[0] % 128 == 0
        )
        args = (tokens_in, cotangent, next_tokens, master, first_moment, second_moment)
        if fits:
            return tuple(fused(n_shard // PAIR, *args))
        return plain(*args)

    spec = P(("replica", "shard"), None)
    return jax.shard_map(
        on_device, mesh=mesh, in_specs=(spec,) * 6, out_specs=(spec,) * 4, check_vma=False
    )
```

time: 49.9 us -> 55 us (1.10)
  Pallas kernels: 40.1 us -> 54.2 us
  local copies, waits for them, and re-layouts: 8.85 us -> 0 us
    pallas_call x1 -> x2, Pallas kernels: 40.1 us -> 54.2 us  [the longest x1 40.6 us: fused(): pl.pallas_call(functools.partial(kernel, Z, own), out_shape=out_shape, in...]
    unnamed x16 -> x0, local copies, waits for them, and re-layouts: 8.85 us -> none
where the time goes in v2:
time: 55 us; the launch traced here: 54.8 us
  Pallas kernels  54.2 us (99%)
  between operations  0.64 us (1%)
    pallas_call x1, Pallas kernels, fused(): pl.pallas_call(functools.partial(kernel, Z, own), out_shape=out_shape, in...  40.6 us
    pallas_call x1, Pallas kernels, fused(): pl.pallas_call(write_out, out_shape=out_shape, in_specs=[any_spec] * 4, o...  13.5 us

profile of v2, /device:TPU:0, one launch (start us, length us, event | category | flops | bytes accessed | tf_op | source)
XLA Modules:
  0.0 54.8 jit_solution(17406444166895979785)
XLA Ops:
  0.6 40.6 %shard_map.93 = (f32[256,128]{1,0:T(8,128)}, f32[256,128]{1,0:T(8,128)}, f32[256,128]{1,0:T(8,128)}, bf16[64,128]{1,0:T(8,128)(2,1)}) custom-call(bf16[128,8192]{1,0:T(8,128)(2,1)} %tok_hbm.1, bf16[128,128]{1,0:T(8,128)(2,1)} %cot_hbm.1, bf16[64,8192]{1,0:T(8,128)(2,1)} %nxt_hbm.1, f32[256,128]{1,0:T(8,128)} %master_hbm.1, f32[256,128]{1,0:T(8,128)} %first_hbm.1, ...), custom_call_target="tpu_custom_call" | custom-call | tf_op jit(solution)/shard_map/pallas_call | solution.py:312
  41.3 13.5 %shard_map.94 = (f32[256,128]{1,0:T(8,128)}, f32[256,128]{1,0:T(8,128)}, f32[256,128]{1,0:T(8,128)}, bf16[64,128]{1,0:T(8,128)(2,1)}) custom-call(f32[256,128]{1,0:T(8,128)} %get-tuple-element.8.a, f32[256,128]{1,0:T(8,128)} %get-tuple-element.9.b, f32[256,128]{1,0:T(8,128)} %get-tuple-element.10.c, bf16[64,128]{1,0:T(8,128)(2,1)} %get-tuple-element.11.d), custom_call_target="tpu_custom_call" | custom-call | tf_op jit(solution)/shard_map/pallas_call | solution.py:322

commit v3 on v2

--- a/solution.py
+++ b/solution.py
@@ -34,9 +34,9 @@
     Z, own,
     tok_hbm, cot_hbm, nxt_hbm, master_hbm, first_hbm, second_hbm,
     nm_out, nf_out, ns_out, out_ref,
-    tok, cot, nxt, state, fresh,
+    tok, cot, ntok, nxt, state, fresh,
     g32, gb, rc, hb, rp, jb, rq, kb, rz, wall, acc, ro,
-    tok_sem, cot_sem, nxt_sem, state_sem, fresh_sem,
+    tok_sem, cot_sem, ntok_sem, nxt_sem, state_sem, fresh_sem,
     n_s, n_r, c_s, c_r, p_s, p_r, q_s, q_r, z_s, z_r,
     az_s, az_r, aq_s, aq_r, o_s, o_r,
 ):
@@ -58,10 +58,6 @@
 
     def z_at(j):
         return at(y, c, (z + j) % Z, x)
-
-    def block_at(h, pp, qq, zz):
-        yy, xx = qq * (1 - h) + pp * h, pp * (1 - h) + qq * h
-        return ((yy * PAIR + h) * Z + zz) * PAIR + xx
 
     sib, p_peer, q_peer = at(y, 1 - c, z, x), over_p(c), over_q(c)
 
@@ -145,60 +141,69 @@
         z_cp[k] = send(kb.at[k], rz.at[k], z_s.at[k], z_r.at[k], z_at(k + 1))
         return None
 
-    swaps, nxt_loads = {}, {}
+    swaps, nxt_loads, ntok_loads = {}, {}, []
+
+    def load_tokens():
+        for yy in range(PAIR):
+            for h in range(PAIR):
+                for zz in range(Z):
+                    cp = pltpu.make_async_copy(
+                        nxt_hbm.at[:, pl.ds(((yy * PAIR + h) * Z + zz) * wide, wide)],
+                        ntok.at[yy, h, zz], ntok_sem.at[yy, h, zz],
+                    )
+                    cp.start()
+                    ntok_loads.append(cp)
+
+    def columns_for(h, pp, qq):
+        yy, xx = qq * (1 - h) + pp * h, pp * (1 - h) + qq * h
+        return ntok.at[yy, h, :, :, pl.ds(pl.multiple_of(xx * own, own), own)]
 
     def swap(i, who):
         h, pp, qq, dev = (
             (1 - c, q, p, sib), (c, 1 - p, q, p_peer), (1 - c, 1 - q, p, over_q(1 - c))
         )[who]
         qq = qq if i == 0 else 1 - qq
-        for j in range(Z):
-            zj = (z - j + Z) % Z
-            col = pl.multiple_of(block_at(h, pp, qq, zj) * own, own)
-            swaps[i, who, j] = send(
-                nxt_hbm.at[:, pl.ds(col, own)], nxt.at[zj, qq, pl.ds((who + 1) * rows, rows)],
-                n_s.at[i, who, j], n_r.at[i, who, j], dev,
-            )
-
-    def local_tokens():
-        for i in range(PAIR):
-            qq = q if i == 0 else 1 - q
-            for j in range(Z):
-                zj = (z - j + Z) % Z
-                col = pl.multiple_of(block_at(c, p, qq, zj) * own, own)
-                cp = pltpu.make_async_copy(
-                    nxt_hbm.at[:, pl.ds(col, own)], nxt.at[zj, qq, pl.ds(0, rows)], nxt_sem.at[i, j]
-                )
-                cp.start()
-                nxt_loads[i, j] = cp
+        swaps[i, who] = send(
+            columns_for(h, pp, qq), nxt.at[qq, :, pl.ds((who + 1) * rows, rows)],
+            n_s.at[i, who], n_r.at[i, who], dev,
+        )
+
+    def local_tokens(i):
+        qq = q if i == 0 else 1 - q
+        nxt_loads[i] = pltpu.make_async_copy(
+            columns_for(c, p, qq), nxt.at[qq, :, pl.ds(0, rows)], nxt_sem.at[i]
+        )
+        nxt_loads[i].start()
 
     state_loads = [
         pltpu.make_async_copy(src, state.at[i], state_sem.at[i])
         for i, src in enumerate((master_hbm, first_hbm, second_hbm))
     ]
     total = None
-    for t in range(Z + 3):
+    for t in range(Z + 4):
         if t < Z:
             stage_core(t)
-            if t == 0:
-                swap(0, 1)
-                swap(0, 2)
             own_terms(t)
         if 0 <= t - 1 < Z:
             stage_p(t - 1)
-        if t == Z:
-            swap(0, 0)
-            swap(1, 0)
-            local_tokens()
+        if t == 1:
+            load_tokens()
             for cp in state_loads:
                 cp.start()
-        if 0 <= t - 2 < Z:
-            stage_q(t - 2)
-        if t == Z + 1:
-            swap(1, 1)
-            swap(1, 2)
+        if t == Z:
+            for cp in ntok_loads:
+                cp.wait()
+            for i in range(PAIR):
+                local_tokens(i)
+                swap(i, 0)
         if 0 <= t - 3 < Z:
-            total = stage_z(t - 3)
+            stage_q(t - 3)
+        if t == Z + 2:
+            for i in range(PAIR):
+                swap(i, 1)
+                swap(i, 2)
+        if 0 <= t - 4 < Z:
+            total = stage_z(t - 4)
 
     for cp in state_loads:
         cp.wait()
@@ -219,10 +224,11 @@
     def product(j, i):
         zj = (z - j + Z) % Z
         qq = q if i == 0 else 1 - q
-        nxt_loads[i, j].wait()
-        for who in range(3):
-            swaps[i, who, j].wait_recv()
-        return jnp.dot(nxt[zj, qq], wall[zj, qq], preferred_element_type=f32)
+        if j == 0:
+            nxt_loads[i].wait()
+            for who in range(3):
+                swaps[i, who].wait_recv()
+        return jnp.dot(nxt[qq, zj], wall[zj, qq], preferred_element_type=f32)
 
     forward(0)
     for i, value in enumerate((new_master, new_first, new_second)):
@@ -259,15 +265,11 @@
         cp.wait_send()
 
 
-def write_out(a, b, c, d, a_out, b_out, c_out, d_out, sem):
-    copies = [
-        pltpu.make_async_copy(src, dst, sem.at[i])
-        for i, (src, dst) in enumerate(((a, a_out), (b, b_out), (c, c_out), (d, d_out)))
-    ]
-    for cp in copies:
-        cp.start()
-    for cp in copies:
-        cp.wait()
+def write_out(a, b, c, d, a_out, b_out, c_out, d_out):
+    a_out[...] = a[...]
+    b_out[...] = b[...]
+    c_out[...] = c[...]
+    d_out[...] = d[...]
 
 
 def fused(Z, tokens_in, cotangent, next_tokens, master, first_moment, second_moment):
@@ -282,7 +284,8 @@
     scratch = [
         pltpu.VMEM((Z, PAIR * PAIR, count, PAIR * own), bf16),
         pltpu.VMEM((count, cols), bf16),
-        pltpu.VMEM((Z, PAIR, 4 * rows, own), bf16),
+        pltpu.VMEM((PAIR, PAIR, Z, rows, PAIR * own), bf16),
+        pltpu.VMEM((PAIR, Z, 4 * rows, own), bf16),
         pltpu.VMEM((3, own, cols), f32),
         pltpu.VMEM((3, own, cols), f32),
         pltpu.VMEM((Z, PAIR, PAIR) + block, f32),
@@ -297,8 +300,8 @@
         pltpu.VMEM((Z, PAIR, own, cols), bf16),
         pltpu.VMEM((4 * rows, cols), f32),
         pltpu.VMEM((3, rows, cols), f32),
-        dma((Z, PAIR * PAIR)), dma, dma((PAIR, Z)), dma((3,)), dma((3,)),
-        dma((PAIR, 3, Z)), dma((PAIR, 3, Z)),
+        dma((Z, PAIR * PAIR)), dma, dma((PAIR, PAIR, Z)), dma((PAIR,)), dma((3,)), dma((3,)),
+        dma((PAIR, 3)), dma((PAIR, 3)),
         dma((Z,)), dma((Z,)), dma((Z,)), dma((Z,)), dma((Z,)), dma((Z,)),
         dma((Z - 1,)), dma((Z - 1,)),
         dma((Z - 1,)), dma((Z - 1,)), dma((Z,)), dma((Z,)), dma((3,)), dma((3,)),
@@ -319,12 +322,12 @@
             collective_id=0, has_side_effects=True, vmem_limit_bytes=VMEM_BYTES
         ),
     )(tokens_in, cotangent, next_tokens, master, first_moment, second_moment)
+    vmem_spec = pl.BlockSpec(memory_space=pltpu.VMEM)
     return pl.pallas_call(
         write_out,
         out_shape=out_shape,
-        in_specs=[any_spec] * 4,
-        out_specs=(hbm_spec,) * 4,
-        scratch_shapes=[dma((4,))],
+        in_specs=[vmem_spec] * 4,
+        out_specs=(vmem_spec,) * 4,
         compiler_params=pltpu.CompilerParams(vmem_limit_bytes=VMEM_BYTES),
     )(*results)
 

time: 55 us -> 40.4 us (0.73)
  Pallas kernels: 54.2 us -> 39.6 us
    pallas_call x1, Pallas kernels: 13.5 us -> 1.79 us  [fused(): pl.pallas_call(write_out, out_shape=out_shape, in_specs=[vmem_spec] * 4,...]
    pallas_call x1, Pallas kernels: 40.6 us -> 37.9 us  [fused(): pl.pallas_call(functools.partial(kernel, Z, own), out_shape=out_shape, in...]
where the time goes in v3:
time: 40.4 us; the launch traced here: 40.3 us
  Pallas kernels  39.6 us (98%)
  between operations  0.64 us (2%)
    pallas_call x1, Pallas kernels, fused(): pl.pallas_call(functools.partial(kernel, Z, own), out_shape=out_shape, in...  37.9 us
    pallas_call x1, Pallas kernels, fused(): pl.pallas_call(write_out, out_shape=out_shape, in_specs=[vmem_spec] * 4,...  1.79 us

profile of v3, /device:TPU:0, one launch (start us, length us, event | category | flops | bytes accessed | tf_op | source)
XLA Modules:
  0.0 40.3 jit_solution(16809982262374006890)
XLA Ops:
  0.6 37.9 %shard_map.93 = (f32[256,128]{1,0:T(8,128)}, f32[256,128]{1,0:T(8,128)}, f32[256,128]{1,0:T(8,128)}, bf16[64,128]{1,0:T(8,128)(2,1)}) custom-call(bf16[128,8192]{1,0:T(8,128)(2,1)} %tok_hbm.1, bf16[128,128]{1,0:T(8,128)(2,1)} %cot_hbm.1, bf16[64,8192]{1,0:T(8,128)(2,1)} %nxt_hbm.1, f32[256,128]{1,0:T(8,128)} %master_hbm.1, f32[256,128]{1,0:T(8,128)} %first_hbm.1, ...), custom_call_target="tpu_custom_call" | custom-call | tf_op jit(solution)/shard_map/pallas_call | solution.py:315
  38.5 1.8 %shard_map.94 = (f32[256,128]{1,0:T(8,128)}, f32[256,128]{1,0:T(8,128)}, f32[256,128]{1,0:T(8,128)}, bf16[64,128]{1,0:T(8,128)(2,1)}) custom-call(f32[256,128]{1,0:T(8,128)} %get-tuple-element.8.a, f32[256,128]{1,0:T(8,128)} %get-tuple-element.9.b, f32[256,128]{1,0:T(8,128)} %get-tuple-element.10.c, bf16[64,128]{1,0:T(8,128)(2,1)} %get-tuple-element.11.d), custom_call_target="tpu_custom_call" | custom-call | tf_op jit(solution)/shard_map/pallas_call | solution.py:326

commit v4 on v3

--- a/solution.py
+++ b/solution.py
@@ -34,9 +34,9 @@
     Z, own,
     tok_hbm, cot_hbm, nxt_hbm, master_hbm, first_hbm, second_hbm,
     nm_out, nf_out, ns_out, out_ref,
-    tok, cot, ntok, nxt, state, fresh,
+    tok, cot, ntok, nxt, state,
     g32, gb, rc, hb, rp, jb, rq, kb, rz, wall, acc, ro,
-    tok_sem, cot_sem, ntok_sem, nxt_sem, state_sem, fresh_sem,
+    tok_sem, cot_sem, ntok_sem, nxt_sem, state_sem,
     n_s, n_r, c_s, c_r, p_s, p_r, q_s, q_r, z_s, z_r,
     az_s, az_r, aq_s, aq_r, o_s, o_r,
 ):
@@ -60,6 +60,12 @@
         return at(y, c, (z + j) % Z, x)
 
     sib, p_peer, q_peer = at(y, 1 - c, z, x), over_p(c), over_q(c)
+
+    barrier = pltpu.get_barrier_semaphore()
+    peers = [sib, p_peer, q_peer, over_p(1 - c), over_q(1 - c)]
+    peers += [z_at(j) for j in range(1, Z)]
+    for d in peers:
+        pl.semaphore_signal(barrier, inc=1, device_id=d, device_id_type=MESH)
 
     loads = []
     cot_load = pltpu.make_async_copy(cot_hbm, cot, cot_sem)
@@ -75,12 +81,6 @@
             cp.start()
             row.append(cp)
         loads.append(row)
-        if k == 0:
-            barrier = pltpu.get_barrier_semaphore()
-            peers = [sib, p_peer, q_peer, over_p(1 - c), over_q(1 - c)]
-            peers += [z_at(j) for j in range(1, Z)]
-            for d in peers:
-                pl.semaphore_signal(barrier, inc=1, device_id=d, device_id_type=MESH)
 
     def send(src, dst, s_sem, r_sem, dev):
         cp = pltpu.make_async_remote_copy(
@@ -209,55 +209,76 @@
         cp.wait()
     for k in range(Z - 1):
         z_cp[k].wait_recv()
-        total = total + rz[k].astype(f32)
-    new_master, new_first, new_second = adam(total.T, state[0], state[1], state[2])
-    wall[z, q] = new_master.astype(bf16)
-
-    az, aq = {}, {}
-    for j in range(1, Z):
-        az[j] = send(wall.at[z, q], wall.at[z, q], az_s.at[j - 1], az_r.at[j - 1], z_at(j))
-
-    def forward(j):
-        zj = (z - j + Z) % Z
-        aq[j] = send(wall.at[zj, q], wall.at[zj, q], aq_s.at[j], aq_r.at[j], q_peer)
-
-    def product(j, i):
+
+    az, aq, stores = {}, {}, []
+    half = own // 2
+
+    def piece(zz, hh):
+        return wall.at[zz, q, pl.ds(hh * half, half)]
+
+    def forward(j, hh):
+        part = piece((z - j + Z) % Z, hh)
+        aq[j, hh] = send(part, part, aq_s.at[j, hh], aq_r.at[j, hh], q_peer)
+
+    for hh in range(2):
+        part = pl.ds(hh * half, half)
+        gradient = total[:, hh * half:(hh + 1) * half]
+        for k in range(Z - 1):
+            gradient = gradient + rz[k, :, part].astype(f32)
+        new_master, new_first, new_second = adam(
+            gradient.T, state[0, part], state[1, part], state[2, part]
+        )
+        wall[z, q, part] = new_master.astype(bf16)
+        for j in range(1, Z):
+            az[j, hh] = send(
+                piece(z, hh), piece(z, hh), az_s.at[j - 1, hh], az_r.at[j - 1, hh], z_at(j)
+            )
+        forward(0, hh)
+        nm_out[part] = new_master
+        nf_out[part] = new_first
+        ns_out[part] = new_second
+
+    def product(j, i, first, count):
         zj = (z - j + Z) % Z
         qq = q if i == 0 else 1 - q
-        if j == 0:
-            nxt_loads[i].wait()
-            for who in range(3):
-                swaps[i, who].wait_recv()
-        return jnp.dot(nxt[qq, zj], wall[zj, qq], preferred_element_type=f32)
-
-    forward(0)
-    for i, value in enumerate((new_master, new_first, new_second)):
-        fresh[i] = value
-    stores = [
-        pltpu.make_async_copy(fresh.at[i], dst, fresh_sem.at[i])
-        for i, dst in enumerate((nm_out, nf_out, ns_out))
-    ]
-    for cp in stores:
-        cp.start()
-    acc[...] = product(0, 0)
+        return jnp.dot(
+            nxt[qq, zj, pl.ds(first, count)], wall[zj, qq], preferred_element_type=f32
+        )
+
+    def tokens_here(i):
+        nxt_loads[i].wait()
+        for who in range(3):
+            swaps[i, who].wait_recv()
+
+    tokens_here(0)
+    acc[...] = product(0, 0, 0, 4 * rows)
     for j in range(1, Z):
-        az[j].wait_recv()
-        forward(j)
-        acc[...] += product(j, 0)
-        aq[j - 1].wait_recv()
-        acc[...] += product(j - 1, 1)
-    aq[Z - 1].wait_recv()
-    acc[...] += product(Z - 1, 1)
-
-    last = [
-        send(acc.at[pl.ds((who + 1) * rows, rows)], ro.at[who], o_s.at[who], o_r.at[who], dev)
-        for who, dev in ((1, p_peer), (2, over_p(1 - c)), (0, sib))
-    ]
+        for hh in range(2):
+            az[j, hh].wait_recv()
+            forward(j, hh)
+        acc[...] += product(j, 0, 0, 4 * rows)
+        if j == 1:
+            tokens_here(1)
+        for hh in range(2):
+            aq[j - 1, hh].wait_recv()
+        acc[...] += product(j - 1, 1, 0, 4 * rows)
+    for hh in range(2):
+        aq[Z - 1, hh].wait_recv()
+
+    far, near = pl.ds(2 * rows, 2 * rows), pl.ds(0, 2 * rows)
+    acc[far] += product(Z - 1, 1, 2 * rows, 2 * rows)
+
+    def part_to(who, dev):
+        return send(
+            acc.at[pl.ds((who + 1) * rows, rows)], ro.at[who], o_s.at[who], o_r.at[who], dev
+        )
+
+    last = [part_to(1, p_peer), part_to(2, over_p(1 - c))]
+    acc[near] += product(Z - 1, 1, 0, 2 * rows)
+    last.append(part_to(0, sib))
     for cps in (core_cp, p_cp, q_cp, z_cp, az, aq, swaps):
         for cp in cps.values():
             cp.wait_send()
-    for cp in stores:
-        cp.wait()
     for cp in last:
         cp.wait_recv()
     out_ref[...] = (acc[pl.ds(0, rows)] + ro[0] + ro[1] + ro[2]).astype(bf16)
@@ -279,14 +300,13 @@
     rows = next_tokens.shape[0]
     dma = pltpu.SemaphoreType.DMA
     block = (cols, own)
-    any_spec = pl.BlockSpec(memory_space=pl.ANY)
+    vmem_spec = pl.BlockSpec(memory_space=pltpu.VMEM)
     hbm_spec = pl.BlockSpec(memory_space=pltpu.HBM)
     scratch = [
         pltpu.VMEM((Z, PAIR * PAIR, count, PAIR * own), bf16),
         pltpu.VMEM((count, cols), bf16),
         pltpu.VMEM((PAIR, PAIR, Z, rows, PAIR * own), bf16),
         pltpu.VMEM((PAIR, Z, 4 * rows, own), bf16),
-        pltpu.VMEM((3, own, cols), f32),
         pltpu.VMEM((3, own, cols), f32),
         pltpu.VMEM((Z, PAIR, PAIR) + block, f32),
         pltpu.VMEM((Z, PAIR, PAIR) + block, bf16),
@@ -300,11 +320,11 @@
         pltpu.VMEM((Z, PAIR, own, cols), bf16),
         pltpu.VMEM((4 * rows, cols), f32),
         pltpu.VMEM((3, rows, cols), f32),
-        dma((Z, PAIR * PAIR)), dma, dma((PAIR, PAIR, Z)), dma((PAIR,)), dma((3,)), dma((3,)),
+        dma((Z, PAIR * PAIR)), dma, dma((PAIR, PAIR, Z)), dma((PAIR,)), dma((3,)),
         dma((PAIR, 3)), dma((PAIR, 3)),
         dma((Z,)), dma((Z,)), dma((Z,)), dma((Z,)), dma((Z,)), dma((Z,)),
         dma((Z - 1,)), dma((Z - 1,)),
-        dma((Z - 1,)), dma((Z - 1,)), dma((Z,)), dma((Z,)), dma((3,)), dma((3,)),
+        dma((Z - 1, 2)), dma((Z - 1, 2)), dma((Z, 2)), dma((Z, 2)), dma((3,)), dma((3,)),
     ]
     out_shape = (
         jax.ShapeDtypeStruct(master.shape, f32),
@@ -314,21 +334,20 @@
     )
     results = pl.pallas_call(
         functools.partial(kernel, Z, own),
-        out_shape=out_shape,
+        out_shape=tuple(pltpu.VMEM(a.shape, a.dtype) for a in out_shape),
         in_specs=[hbm_spec] * 6,
-        out_specs=(any_spec, any_spec, any_spec, pl.BlockSpec(memory_space=pltpu.VMEM)),
+        out_specs=(vmem_spec,) * 4,
         scratch_shapes=scratch,
         compiler_params=pltpu.CompilerParams(
             collective_id=0, has_side_effects=True, vmem_limit_bytes=VMEM_BYTES
         ),
     )(tokens_in, cotangent, next_tokens, master, first_moment, second_moment)
-    vmem_spec = pl.BlockSpec(memory_space=pltpu.VMEM)
     return pl.pallas_call(
         write_out,
         out_shape=out_shape,
         in_specs=[vmem_spec] * 4,
         out_specs=(vmem_spec,) * 4,
-        compiler_params=pltpu.CompilerParams(vmem_limit_bytes=VMEM_BYTES),
+        compiler_params=pltpu.CompilerParams(vmem_limit_bytes=VMEM_BYTES // 8),
     )(*results)
 
 
@@ -369,7 +388,7 @@
             n_rep == PAIR * PAIR
             and n_shard % PAIR == 0
             and n_shard > PAIR
-            and own % 128 == 0
+            and own % 256 == 0
             and cols % 128 == 0
             and next_tokens.shape[0] % 16 == 0
             and tokens_in.shape[0] % 128 == 0

time: 40.4 us -> 39.1 us (0.968)
  Pallas kernels: 39.6 us -> 38.2 us
    pallas_call x1, Pallas kernels: 1.79 us -> 0.77 us  [fused(): pl.pallas_call(write_out, out_shape=out_shape, in_specs=[vmem_spec] * 4,...]
where the time goes in v4:
time: 39.1 us; the launch traced here: 38.9 us
  Pallas kernels  38.2 us (98%)
  between operations  0.64 us (2%)
    pallas_call x1, Pallas kernels, fused(): pl.pallas_call(functools.partial(kernel, Z, own), out_shape=tuple((pltpu....  37.5 us

profile of v4, /device:TPU:0, one launch (start us, length us, event | category | flops | bytes accessed | tf_op | source)
XLA Modules:
  0.0 38.9 jit_solution(16200309809952696900)
XLA Ops:
  0.6 37.5 %shard_map.93 = (f32[256,128]{1,0:T(8,128)S(1)}, f32[256,128]{1,0:T(8,128)S(1)}, f32[256,128]{1,0:T(8,128)S(1)}, bf16[64,128]{1,0:T(8,128)(2,1)S(1)}) custom-call(bf16[128,8192]{1,0:T(8,128)(2,1)} %tok_hbm.1, bf16[128,128]{1,0:T(8,128)(2,1)} %cot_hbm.1, bf16[64,8192]{1,0:T(8,128)(2,1)} %nxt_hbm.1, f32[256,128]{1,0:T(8,128)} %master_hbm.1, ...), custom_call_target="tpu_custom_call" | custom-call | tf_op jit(solution)/shard_map/pallas_call | solution.py:335
  38.1 0.8 %shard_map.94 = (f32[256,128]{1,0:T(8,128)}, f32[256,128]{1,0:T(8,128)}, f32[256,128]{1,0:T(8,128)}, bf16[64,128]{1,0:T(8,128)(2,1)}) custom-call(f32[256,128]{1,0:T(8,128)S(1)} %get-tuple-element.8.a, f32[256,128]{1,0:T(8,128)S(1)} %get-tuple-element.9.b, f32[256,128]{1,0:T(8,128)S(1)} %get-tuple-element.10.c, bf16[64,128]{1,0:T(8,128)(2,1)S(1)} %get-tuple-element.11.d), custom_call_target="tpu_custom_call" | custom-call | tf_op jit(solution)/shard_map/pallas_call | solution.py:345

commit v5 on v4

--- a/solution.py
+++ b/solution.py
@@ -56,8 +56,16 @@
     def over_q(cc):
         return at((1 - y) * (1 - c) + y * c, cc, z, x * (1 - c) + (1 - x) * c)
 
-    def z_at(j):
-        return at(y, c, (z + j) % Z, x)
+    def z_of(d):
+        zz, bit = z, 1
+        while bit < Z:
+            if d & bit:
+                zz = zz + bit - 2 * bit * ((zz // bit) % 2)
+            bit *= 2
+        return zz
+
+    def z_at(d):
+        return at(y, c, z_of(d), x)
 
     sib, p_peer, q_peer = at(y, 1 - c, z, x), over_p(c), over_q(c)
 
@@ -67,11 +75,11 @@
     for d in peers:
         pl.semaphore_signal(barrier, inc=1, device_id=d, device_id_type=MESH)
 
-    loads = []
+    loads, ntok_loads = [], []
     cot_load = pltpu.make_async_copy(cot_hbm, cot, cot_sem)
     cot_load.start()
     for k in range(Z):
-        zc = (z + 1 + k) % Z
+        zc = z_of(Z - 1 - k)
         row = []
         for yc in range(PAIR * PAIR):
             col = pl.multiple_of((yc * Z + zc) * wide, own)
@@ -81,6 +89,16 @@
             cp.start()
             row.append(cp)
         loads.append(row)
+        if k == 0:
+            for yy in range(PAIR):
+                for h in range(PAIR):
+                    for zz in range(Z):
+                        cp = pltpu.make_async_copy(
+                            nxt_hbm.at[:, pl.ds(((yy * PAIR + h) * Z + zz) * wide, wide)],
+                            ntok.at[yy, h, zz], ntok_sem.at[yy, h, zz],
+                        )
+                        cp.start()
+                        ntok_loads.append(cp)
 
     def send(src, dst, s_sem, r_sem, dev):
         cp = pltpu.make_async_remote_copy(
@@ -138,21 +156,10 @@
         if k == Z - 1:
             return total
         kb[k] = total.astype(bf16)
-        z_cp[k] = send(kb.at[k], rz.at[k], z_s.at[k], z_r.at[k], z_at(k + 1))
+        z_cp[k] = send(kb.at[k], rz.at[k], z_s.at[k], z_r.at[k], z_at(Z - 1 - k))
         return None
 
-    swaps, nxt_loads, ntok_loads = {}, {}, []
-
-    def load_tokens():
-        for yy in range(PAIR):
-            for h in range(PAIR):
-                for zz in range(Z):
-                    cp = pltpu.make_async_copy(
-                        nxt_hbm.at[:, pl.ds(((yy * PAIR + h) * Z + zz) * wide, wide)],
-                        ntok.at[yy, h, zz], ntok_sem.at[yy, h, zz],
-                    )
-                    cp.start()
-                    ntok_loads.append(cp)
+    swaps, nxt_loads = {}, {}
 
     def columns_for(h, pp, qq):
         yy, xx = qq * (1 - h) + pp * h, pp * (1 - h) + qq * h
@@ -183,25 +190,26 @@
     for t in range(Z + 4):
         if t < Z:
             stage_core(t)
+            if t == 0:
+                for cp in ntok_loads:
+                    cp.wait()
+                swap(0, 1)
+                swap(0, 2)
             own_terms(t)
         if 0 <= t - 1 < Z:
             stage_p(t - 1)
         if t == 1:
-            load_tokens()
             for cp in state_loads:
                 cp.start()
         if t == Z:
-            for cp in ntok_loads:
-                cp.wait()
             for i in range(PAIR):
                 local_tokens(i)
                 swap(i, 0)
         if 0 <= t - 3 < Z:
             stage_q(t - 3)
         if t == Z + 2:
-            for i in range(PAIR):
-                swap(i, 1)
-                swap(i, 2)
+            swap(1, 1)
+            swap(1, 2)
         if 0 <= t - 4 < Z:
             total = stage_z(t - 4)
 
@@ -217,7 +225,7 @@
         return wall.at[zz, q, pl.ds(hh * half, half)]
 
     def forward(j, hh):
-        part = piece((z - j + Z) % Z, hh)
+        part = piece(z_of(j), hh)
         aq[j, hh] = send(part, part, aq_s.at[j, hh], aq_r.at[j, hh], q_peer)
 
     for hh in range(2):
@@ -229,7 +237,7 @@
             gradient.T, state[0, part], state[1, part], state[2, part]
         )
         wall[z, q, part] = new_master.astype(bf16)
-        for j in range(1, Z):
+        for j in range(Z - 1, 0, -1):
             az[j, hh] = send(
                 piece(z, hh), piece(z, hh), az_s.at[j - 1, hh], az_r.at[j - 1, hh], z_at(j)
             )
@@ -239,7 +247,7 @@
         ns_out[part] = new_second
 
     def product(j, i, first, count):
-        zj = (z - j + Z) % Z
+        zj = z_of(j)
         qq = q if i == 0 else 1 - q
         return jnp.dot(
             nxt[qq, zj, pl.ds(first, count)], wall[zj, qq], preferred_element_type=f32
@@ -250,23 +258,32 @@
         for who in range(3):
             swaps[i, who].wait_recv()
 
-    tokens_here(0)
-    acc[...] = product(0, 0, 0, 4 * rows)
-    for j in range(1, Z):
+    order = [0] + list(range(Z - 1, 0, -1))
+
+    def second(n):
         for hh in range(2):
-            az[j, hh].wait_recv()
-            forward(j, hh)
-        acc[...] += product(j, 0, 0, 4 * rows)
-        if j == 1:
+            aq[order[n], hh].wait_recv()
+        return product(order[n], 1, 0, 4 * rows)
+
+    for n in range(1, Z):
+        for hh in range(2):
+            az[order[n], hh].wait_recv()
+            forward(order[n], hh)
+        if n == 1:
+            tokens_here(0)
+            acc[...] = product(0, 0, 0, 4 * rows)
+        if n == 2:
             tokens_here(1)
-        for hh in range(2):
-            aq[j - 1, hh].wait_recv()
-        acc[...] += product(j - 1, 1, 0, 4 * rows)
+        acc[...] += product(order[n], 0, 0, 4 * rows)
+        if n >= 2:
+            acc[...] += second(n - 2)
+    acc[...] += second(Z - 2)
+    end = order[Z - 1]
     for hh in range(2):
-        aq[Z - 1, hh].wait_recv()
+        aq[end, hh].wait_recv()
 
     far, near = pl.ds(2 * rows, 2 * rows), pl.ds(0, 2 * rows)
-    acc[far] += product(Z - 1, 1, 2 * rows, 2 * rows)
+    acc[far] += product(end, 1, 2 * rows, 2 * rows)
 
     def part_to(who, dev):
         return send(
@@ -274,7 +291,7 @@
         )
 
     last = [part_to(1, p_peer), part_to(2, over_p(1 - c))]
-    acc[near] += product(Z - 1, 1, 0, 2 * rows)
+    acc[near] += product(end, 1, 0, 2 * rows)
     last.append(part_to(0, sib))
     for cps in (core_cp, p_cp, q_cp, z_cp, az, aq, swaps):
         for cp in cps.values():
@@ -387,7 +404,8 @@
         fits = (
             n_rep == PAIR * PAIR
             and n_shard % PAIR == 0
-            and n_shard > PAIR
+            and n_shard // PAIR > 2
+            and (n_shard // PAIR) & (n_shard // PAIR - 1) == 0
             and own % 256 == 0
             and cols % 128 == 0
             and next_tokens.shape[0] % 16 == 0

time: 39.1 us -> 39 us (level)
  no operation moved by 1% of the time
where the time goes in v5:
time: 39 us; the launch traced here: 38.8 us
  Pallas kernels  38.2 us (98%)
  between operations  0.64 us (2%)
    pallas_call x1, Pallas kernels, fused(): pl.pallas_call(functools.partial(kernel, Z, own), out_shape=tuple((pltpu....  37.4 us

profile of v5, /device:TPU:0, one launch (start us, length us, event | category | flops | bytes accessed | tf_op | source)
XLA Modules:
  0.0 38.8 jit_solution(16602717232270416987)
XLA Ops:
  0.6 37.4 %shard_map.93 = (f32[256,128]{1,0:T(8,128)S(1)}, f32[256,128]{1,0:T(8,128)S(1)}, f32[256,128]{1,0:T(8,128)S(1)}, bf16[64,128]{1,0:T(8,128)(2,1)S(1)}) custom-call(bf16[128,8192]{1,0:T(8,128)(2,1)} %tok_hbm.1, bf16[128,128]{1,0:T(8,128)(2,1)} %cot_hbm.1, bf16[64,8192]{1,0:T(8,128)(2,1)} %nxt_hbm.1, f32[256,128]{1,0:T(8,128)} %master_hbm.1, ...), custom_call_target="tpu_custom_call" | custom-call | tf_op jit(solution)/shard_map/pallas_call | solution.py:352
  38.1 0.8 %shard_map.94 = (f32[256,128]{1,0:T(8,128)}, f32[256,128]{1,0:T(8,128)}, f32[256,128]{1,0:T(8,128)}, bf16[64,128]{1,0:T(8,128)(2,1)}) custom-call(f32[256,128]{1,0:T(8,128)S(1)} %get-tuple-element.8.a, f32[256,128]{1,0:T(8,128)S(1)} %get-tuple-element.9.b, f32[256,128]{1,0:T(8,128)S(1)} %get-tuple-element.10.c, bf16[64,128]{1,0:T(8,128)(2,1)S(1)} %get-tuple-element.11.d), custom_call_target="tpu_custom_call" | custom-call | tf_op jit(solution)/shard_map/pallas_call | solution.py:362

commit v6 on v5

--- a/solution.py
+++ b/solution.py
@@ -138,21 +138,23 @@
 
     def stage_p(k):
         core_cp[k].wait_recv()
-        for qq in range(PAIR):
-            hb[k, qq] = (g32[k, 1 - p, qq] + rc[k, 1 - p, qq].astype(f32)).astype(bf16)
-        p_cp[k] = send(hb.at[k], rp.at[k], p_s.at[k], p_r.at[k], p_peer)
-
-    def partial(k, qq):
-        return g32[k, p, qq] + rc[k, p, qq].astype(f32) + rp[k, qq].astype(f32)
+        for i, qq in enumerate((1 - q, q)):
+            hb[k, i] = (g32[k, 1 - p, qq] + rc[k, 1 - p, qq].astype(f32)).astype(bf16)
+            p_cp[k, i] = send(hb.at[k, i], rp.at[k, i], p_s.at[k, i], p_r.at[k, i], p_peer)
+
+    def partial(k, i):
+        qq = (1 - q, q)[i]
+        p_cp[k, i].wait_recv()
+        return g32[k, p, qq] + rc[k, p, qq].astype(f32) + rp[k, i].astype(f32)
 
     def stage_q(k):
-        p_cp[k].wait_recv()
-        jb[k] = partial(k, 1 - q).astype(bf16)
+        jb[k] = partial(k, 0).astype(bf16)
         q_cp[k] = send(jb.at[k], rq.at[k], q_s.at[k], q_r.at[k], q_peer)
 
     def stage_z(k):
+        total = partial(k, 1)
         q_cp[k].wait_recv()
-        total = partial(k, q) + rq[k].astype(f32)
+        total = total + rq[k].astype(f32)
         if k == Z - 1:
             return total
         kb[k] = total.astype(bf16)
@@ -195,9 +197,10 @@
                     cp.wait()
                 swap(0, 1)
                 swap(0, 2)
-            own_terms(t)
         if 0 <= t - 1 < Z:
             stage_p(t - 1)
+        if t < Z:
+            own_terms(t)
         if t == 1:
             for cp in state_loads:
                 cp.start()
@@ -339,7 +342,7 @@
         pltpu.VMEM((3, rows, cols), f32),
         dma((Z, PAIR * PAIR)), dma, dma((PAIR, PAIR, Z)), dma((PAIR,)), dma((3,)),
         dma((PAIR, 3)), dma((PAIR, 3)),
-        dma((Z,)), dma((Z,)), dma((Z,)), dma((Z,)), dma((Z,)), dma((Z,)),
+        dma((Z,)), dma((Z,)), dma((Z, PAIR)), dma((Z, PAIR)), dma((Z,)), dma((Z,)),
         dma((Z - 1,)), dma((Z - 1,)),
         dma((Z - 1, 2)), dma((Z - 1, 2)), dma((Z, 2)), dma((Z, 2)), dma((3,)), dma((3,)),
     ]

time: 39 us -> 38.8 us (level)
  no operation moved by 1% of the time
where the time goes in v6:
time: 38.8 us; the launch traced here: 38.7 us
  Pallas kernels  38 us (98%)
  between operations  0.64 us (2%)
    pallas_call x1, Pallas kernels, fused(): pl.pallas_call(functools.partial(kernel, Z, own), out_shape=tuple((pltpu....  37.2 us

profile of v6, /device:TPU:0, one launch (start us, length us, event | category | flops | bytes accessed | tf_op | source)
XLA Modules:
  0.0 38.7 jit_solution(12675794211768939007)
XLA Ops:
  0.6 37.2 %shard_map.93 = (f32[256,128]{1,0:T(8,128)S(1)}, f32[256,128]{1,0:T(8,128)S(1)}, f32[256,128]{1,0:T(8,128)S(1)}, bf16[64,128]{1,0:T(8,128)(2,1)S(1)}) custom-call(bf16[128,8192]{1,0:T(8,128)(2,1)} %tok_hbm.1, bf16[128,128]{1,0:T(8,128)(2,1)} %cot_hbm.1, bf16[64,8192]{1,0:T(8,128)(2,1)} %nxt_hbm.1, f32[256,128]{1,0:T(8,128)} %master_hbm.1, ...), custom_call_target="tpu_custom_call" | custom-call | tf_op jit(solution)/shard_map/pallas_call | solution.py:355
  37.9 0.8 %shard_map.94 = (f32[256,128]{1,0:T(8,128)}, f32[256,128]{1,0:T(8,128)}, f32[256,128]{1,0:T(8,128)}, bf16[64,128]{1,0:T(8,128)(2,1)}) custom-call(f32[256,128]{1,0:T(8,128)S(1)} %get-tuple-element.8.a, f32[256,128]{1,0:T(8,128)S(1)} %get-tuple-element.9.b, f32[256,128]{1,0:T(8,128)S(1)} %get-tuple-element.10.c, bf16[64,128]{1,0:T(8,128)(2,1)S(1)} %get-tuple-element.11.d), custom_call_target="tpu_custom_call" | custom-call | tf_op jit(solution)/shard_map/pallas_call | solution.py:365

commit v7 on v6

--- a/solution.py
+++ b/solution.py
@@ -262,6 +262,9 @@
             swaps[i, who].wait_recv()
 
     order = [0] + list(range(Z - 1, 0, -1))
+    for cps in (core_cp, p_cp, q_cp, z_cp):
+        for cp in cps.values():
+            cp.wait_send()
 
     def second(n):
         for hh in range(2):
@@ -277,6 +280,8 @@
             acc[...] = product(0, 0, 0, 4 * rows)
         if n == 2:
             tokens_here(1)
+            for cp in swaps.values():
+                cp.wait_send()
         acc[...] += product(order[n], 0, 0, 4 * rows)
         if n >= 2:
             acc[...] += second(n - 2)
@@ -296,7 +301,7 @@
     last = [part_to(1, p_peer), part_to(2, over_p(1 - c))]
     acc[near] += product(end, 1, 0, 2 * rows)
     last.append(part_to(0, sib))
-    for cps in (core_cp, p_cp, q_cp, z_cp, az, aq, swaps):
+    for cps in (az, aq):
         for cp in cps.values():
             cp.wait_send()
     for cp in last:

time: 38.8 us -> 38.8 us (level)
  no operation moved by 1% of the time
where the time goes in v7:
time: 38.8 us; the launch traced here: 38.7 us
  Pallas kernels  38 us (98%)
  between operations  0.64 us (2%)
    pallas_call x1, Pallas kernels, fused(): pl.pallas_call(functools.partial(kernel, Z, own), out_shape=tuple((pltpu....  37.2 us

profile of v7, /device:TPU:0, one launch (start us, length us, event | category | flops | bytes accessed | tf_op | source)
XLA Modules:
  0.0 38.7 jit_solution(584830035680322198)
XLA Ops:
  0.6 37.2 %shard_map.93 = (f32[256,128]{1,0:T(8,128)S(1)}, f32[256,128]{1,0:T(8,128)S(1)}, f32[256,128]{1,0:T(8,128)S(1)}, bf16[64,128]{1,0:T(8,128)(2,1)S(1)}) custom-call(bf16[128,8192]{1,0:T(8,128)(2,1)} %tok_hbm.1, bf16[128,128]{1,0:T(8,128)(2,1)} %cot_hbm.1, bf16[64,8192]{1,0:T(8,128)(2,1)} %nxt_hbm.1, f32[256,128]{1,0:T(8,128)} %master_hbm.1, ...), custom_call_target="tpu_custom_call" | custom-call | tf_op jit(solution)/shard_map/pallas_call | solution.py:360
  37.9 0.8 %shard_map.94 = (f32[256,128]{1,0:T(8,128)}, f32[256,128]{1,0:T(8,128)}, f32[256,128]{1,0:T(8,128)}, bf16[64,128]{1,0:T(8,128)(2,1)}) custom-call(f32[256,128]{1,0:T(8,128)S(1)} %get-tuple-element.8.a, f32[256,128]{1,0:T(8,128)S(1)} %get-tuple-element.9.b, f32[256,128]{1,0:T(8,128)S(1)} %get-tuple-element.10.c, bf16[64,128]{1,0:T(8,128)(2,1)S(1)} %get-tuple-element.11.d), custom_call_target="tpu_custom_call" | custom-call | tf_op jit(solution)/shard_map/pallas_call | solution.py:370
